TPU v7x, 256 devices: a whole 4x4x8 slice. The times are simulated.
256 devices in a mesh: dp: 64 (over y, z, core), mp: 4 (over x).
Axes of the slice: x: 4, y: 4, z: 8, core: 2. Of those that a mesh axis runs over, the one named last changes fastest.
Arguments:
- pool: bfloat16 [4096, 36864], P('dp', 'mp'), may hold values from -6 to 6
- send_slots: int32 [64, 64], P('dp'), may hold values from 0 to 63, each once within a row
- page_source: int32 [64, 40], P('dp'), may hold values from 0 to 63, as said below
- prefix_pages: int32 [64], P('dp'), may hold values from 10 to 40, as said below
- queries: bfloat16 [4096, 73728], P('dp', 'mp'), may hold values from -50 to 50
- suffix_kv: bfloat16 [4096, 576], P('dp'), may hold values from -6 to 6
- hidden_in: bfloat16 [4096, 7168], P('dp', 'mp'), may hold values from -6 to 6
- expert_ids: int32 [4096, 8], P('dp'), may hold values from 0 to 255, as said below
- expert_slots: int32 [4096, 8], P('dp'), may hold values from -1 to 3, as said below
- gate_weights: float32 [4096, 8], P('dp'), may hold values from 0.05 to 0.4
- w_gate_up: bfloat16 [64, 7168, 1024], P('dp', 'mp'), may hold values from -0.0625 to 0.0625
- w_down: bfloat16 [64, 512, 7168], P('dp', None, 'mp'), may hold values from -0.1875 to 0.1875
Outputs:
- context: bfloat16 [4096, 65536], P('dp', 'mp')
- moe_out: bfloat16 [4096, 7168], P('dp', 'mp')
Inputs may be any that keep to these rules, and one draw needn't show every extreme that they name: `send_slots`: each row orders all 64 slots of the group's store. `page_source`: entry s + c: the page is position c of what group s sends to the request's group; no entry repeats within a row. `prefix_pages`: some group's request has exactly 40 pages. `expert_ids`: each row names 8 different experts. `expert_slots`: a live slot belongs to an id below 32; one group's assignments to one expert take slots 0, 1, 2 and so on in token order, and -1 marks ids of 32 or more and assignments past 4; in every draw some expert receives 4 rows from every group.
All inputs are finite; a program needn't handle non-finite values.
Results may differ from a plain program's by a relative error of at most 0.027.
Values may be sent and summed in bfloat16 or wider, within the bound.
A program may use at most 128 MiB of HBM per device.

v0:
```python
import jax
import jax.numpy as jnp
from jax import lax
from jax.sharding import PartitionSpec as P

KVL = 512
PAGE = 64
CAP = 4


score_scale = 192 ** (-0.5)
very_low = -1e30


def absorb_block(state, local_queries, key_rows, visible, latent):
    peak, totals, summed = state
    scores = (
        jnp.einsum("qhc,kc->qhk", local_queries, key_rows, preferred_element_type=jnp.float32)
        * score_scale
    )
    scores = jnp.where(visible, scores, very_low)
    new_peak = jnp.maximum(peak, jnp.max(scores, axis=-1))
    weights = jnp.where(visible, jnp.exp(scores - new_peak[..., None]), 0.0)
    factor = jnp.exp(peak - new_peak)
    totals = totals * factor + jnp.sum(weights, axis=-1)
    summed = summed * factor[..., None] + jnp.einsum(
        "qhk,kc->qhc",
        weights.astype(jnp.bfloat16),
        key_rows[:, :latent],
        preferred_element_type=jnp.float32,
    )
    return (new_peak, totals, summed)


def attend(local_queries, prefix_keys, suffix_keys, live_limit, latent):
    row_count, head_count, entries = local_queries.shape
    key_count = prefix_keys.shape[0]
    key_block = min(512, key_count)
    start_state = (
        jnp.full((row_count, head_count), very_low, jnp.float32),
        jnp.zeros((row_count, head_count), jnp.float32),
        jnp.zeros((row_count, head_count, latent), jnp.float32),
    )

    def visit_block(state, step_index):
        offset = step_index * key_block
        key_rows = lax.dynamic_slice_in_dim(prefix_keys, offset, key_block, 0)
        visible = offset + jnp.arange(key_block) < live_limit
        return (absorb_block(state, local_queries, key_rows, visible[None, None, :], latent), None)

    state, unused = lax.scan(visit_block, start_state, jnp.arange(key_count // key_block))
    causal = jnp.arange(row_count)[None, :] <= jnp.arange(row_count)[:, None]
    peak, totals, summed = absorb_block(
        state, local_queries, suffix_keys, causal[:, None, :], latent
    )
    return (summed / totals[..., None]).astype(jnp.bfloat16)


def body(
    pool,
    send_slots,
    page_source,
    prefix_pages,
    queries,
    suffix_kv,
    hidden_in,
    expert_ids,
    expert_slots,
    gate_weights,
    w_gate_up,
    w_down,
):
    groups = lax.axis_size("dp")
    row_width = pool.shape[1]
    ordered = jnp.take(pool, send_slots[0], axis=0)
    arrived = lax.all_to_all(
        ordered.reshape(groups, -1, row_width), "dp", split_axis=0, concat_axis=0, tiled=True
    )
    arrived = arrived.reshape(-1, row_width)
    source = page_source[0]
    page_rows = jnp.take(lax.all_gather(arrived, "mp", axis=1, tiled=True), source, axis=0)
    entries = suffix_kv.shape[1]
    prefix_keys = page_rows.reshape(-1, entries)
    row_count = queries.shape[0]
    head_count = queries.shape[1] // entries
    local_queries = queries.reshape(row_count, head_count, entries)
    context = attend(local_queries, prefix_keys, suffix_kv, prefix_pages[0] * PAGE, KVL)
    context = context.reshape(row_count, head_count * KVL)
    experts_here = groups // 2
    slot_count = experts_here * CAP
    quarter = hidden_in.shape[1]
    target = expert_ids * CAP + expert_slots
    columns = jnp.arange(slot_count)
    matches = (target[:, :, None] == columns) & (expert_slots >= 0)[:, :, None]
    select = jnp.any(matches, axis=1).astype(jnp.bfloat16)
    picked = jnp.einsum("ts,td->sd", select, hidden_in, preferred_element_type=jnp.float32).astype(
        jnp.bfloat16
    )
    paired = jnp.broadcast_to(
        picked.reshape(experts_here, 1, CAP, quarter), (experts_here, 2, CAP, quarter)
    ).reshape(groups, CAP, quarter)
    received = lax.all_to_all(paired, "dp", split_axis=0, concat_axis=0, tiled=True).reshape(
        groups * CAP, quarter
    )
    preacts = jnp.dot(received, w_gate_up[0], preferred_element_type=jnp.float32)
    half_units = preacts.shape[1] // 2
    preacts = lax.psum(preacts.astype(jnp.bfloat16), "mp").astype(jnp.float32)
    hidden = (jax.nn.silu(preacts[:, :half_units]) * preacts[:, half_units:]).astype(jnp.bfloat16)
    pair_part = jnp.dot(hidden, w_down[0], preferred_element_type=jnp.float32)
    returned = lax.all_to_all(
        pair_part.reshape(groups, CAP, quarter).astype(jnp.bfloat16),
        "dp",
        split_axis=0,
        concat_axis=0,
        tiled=True,
    ).astype(jnp.float32)
    returned = returned.reshape(experts_here, 2, CAP, quarter)
    outputs = (returned[:, 0] + returned[:, 1]).astype(jnp.bfloat16).reshape(slot_count, quarter)
    weights = jnp.sum(jnp.where(matches, gate_weights[:, :, None], 0.0), axis=1)
    mixed = jnp.dot(weights, outputs.astype(jnp.float32), precision=lax.Precision.HIGHEST)
    return (context, mixed.astype(jnp.bfloat16))


def solution(mesh):
    return jax.shard_map(
        body,
        mesh=mesh,
        in_specs=(
            P("dp", "mp"),
            P("dp", None),
            P("dp", None),
            P("dp"),
            P("dp", "mp"),
            P("dp", None),
            P("dp", "mp"),
            P("dp", None),
            P("dp", None),
            P("dp", None),
            P("dp", "mp", None),
            P("dp", None, "mp"),
        ),
        out_specs=(P("dp", "mp"), P("dp", "mp")),
        check_vma=False,
    )
```

profile of v0, /device:TPU:1, one launch (start us, length us, event | category | flops | bytes accessed | tf_op | source)
XLA Modules:
  0.0 274.1 jit_solution(1293134772099168151)
XLA Ops:
  10.3 1.3 convolution_convert_fusion.1
  11.6 0.9 broadcast_in_dim.119
  12.5 2.2 broadcast_in_dim.120
  14.7 13.3 %all-to-all-start.1 = ((bf16[64,4,1792]{2,1,0:T(4,128)(2,1)}), bf16[64,4,1792]{2,1,0:T(4,128)(2,1)}, u32[]{:S(2)}, u32[]{:S(2)}) async-start(bf16[64,4,1792]{2,1,0:T(4,128)(2,1)} %bitcast.90), calls=%async_computation.1 | async-start | bytes 1835008 | tf_op jit(solution)/shard_map/all_to_all | solution.py:102
  28.0 2.3 gather_fusion
  30.3 1.4 bitcast_select_fusion
  32.3 2.2 reduce
  34.5 2.8 %reshape.188 = bf16[64,2,4608]{2,1,0:T(2,128)(2,1)} reshape(bf16[64,9216]{1,0:T(8,128)(2,1)} %reduce) | data formatting | bytes 2359296
  37.2 16.4 %all-to-all-done.1 = bf16[64,4,1792]{2,1,0:T(4,128)(2,1)} async-done(((bf16[64,4,1792]{2,1,0:T(4,128)(2,1)}), bf16[64,4,1792]{2,1,0:T(4,128)(2,1)}, u32[]{:S(2)}, u32[]{:S(2)}) %all-to-all-start.1) | async-done | bytes 917536 | tf_op jit(solution)/shard_map/all_to_all | solution.py:102
  53.7 6.2 %all-to-all-start = ((bf16[64,2,4608]{2,1,0:T(2,128)(2,1)}), bf16[64,2,4608]{2,1,0:T(2,128)(2,1)S(1)}, u32[]{:S(2)}, u32[]{:S(2)}) async-start(bf16[64,2,4608]{2,1,0:T(2,128)(2,1)} %reshape.188), calls=%async_computation | async-start | bytes 2359296 | tf_op jit(solution)/shard_map/all_to_all | solution.py:76
  59.9 2.4 reshape.161
  62.3 4.3 %fusion.16 = bf16[256,1024]{1,0:T(8,128)(2,1)} fusion(bf16[256,1792]{1,0:T(8,128)(2,1)} %reshape.161, bf16[1,1792,1024]{2,1,0:T(8,128)(2,1)} %param.24), kind=kOutput, calls=%fused_computation.33 | convolution fusion | flops 939786240 | bytes 5111808 | tf_op jit(solution)/shard_map/dot_general | solution.py:105
  66.7 24.6 %all-to-all-done = bf16[64,2,4608]{2,1,0:T(2,128)(2,1)S(1)} async-done(((bf16[64,2,4608]{2,1,0:T(2,128)(2,1)}), bf16[64,2,4608]{2,1,0:T(2,128)(2,1)S(1)}, u32[]{:S(2)}, u32[]{:S(2)}) %all-to-all-start) | async-done | bytes 1179680 | tf_op jit(solution)/shard_map/all_to_all | solution.py:76
  91.3 3.4 %reshape.189 = bf16[64,1,9216]{2,1,0:T(2,128)(2,1)} reshape(bf16[64,2,4608]{2,1,0:T(2,128)(2,1)S(1)} %all-to-all-done) | data formatting | bytes 2359296
  94.7 3.1 %copy.61 = bf16[64,1,9216]{2,0,1:T(8,128)(2,1)} copy(bf16[64,1,9216]{2,1,0:T(2,128)(2,1)} %reshape.189) | data formatting | bytes 2359296 | tf_op jit(solution)/shard_map/all_to_all | solution.py:76
  97.7 16.1 %all-reduce.2.cloned.1.call-done = bf16[256,1024]{1,0:T(8,128)(2,1)} async-done(((bf16[256,1024]{1,0:T(8,128)(2,1)}), bf16[256,1024]{1,0:T(8,128)(2,1)}) %all-reduce.2.cloned.1.call-update) | async-done | bytes 524304 | tf_op jit(solution)/shard_map/psum | solution.py:107
  113.9 1.1 convert_element_type.41
  115.9 1.6 copy.71
  117.6 12.5 %all-to-all-start.2 = ((bf16[64,4,1792]{2,1,0:T(4,128)(2,1)}), bf16[64,4,1792]{2,1,0:T(4,128)(2,1)S(1)}, u32[]{:S(2)}, u32[]{:S(2)}) async-start(bf16[64,4,1792]{2,1,0:T(4,128)(2,1)} %copy.71), calls=%async_computation.2 | async-start | bytes 1835008 | tf_op jit(solution)/shard_map/all_to_all | solution.py:110
  132.2 4.5 %reshape.158 = bf16[64,32,576]{2,1,0:T(8,128)(2,1)S(1)} reshape(bf16[64,18432]{1,0:T(8,128)(2,1)} %param.18) | data formatting | bytes 4718592 | tf_op jit(solution)/shard_map/reshape | solution.py:86
  136.8 2.4 copy.63
  139.9 0.9 select_reduce_fusion
  140.8 2.4 fusion.37
  143.2 12.6 %all-to-all-done.2 = bf16[64,4,1792]{2,1,0:T(4,128)(2,1)S(1)} async-done(((bf16[64,4,1792]{2,1,0:T(4,128)(2,1)}), bf16[64,4,1792]{2,1,0:T(4,128)(2,1)S(1)}, u32[]{:S(2)}, u32[]{:S(2)}) %all-to-all-start.2) | async-done | bytes 917536 | tf_op jit(solution)/shard_map/all_to_all | solution.py:110
  156.6 1.0 convolution_convert_fusion.2
  157.6 16.3 %all-gather.3.cloned.1.call-done = bf16[64,1,36864]{2,0,1:T(8,128)(2,1)} async-done(((bf16[64,1,9216]{2,0,1:T(8,128)(2,1)}), bf16[64,1,36864]{2,0,1:T(8,128)(2,1)}) %all-gather.3.cloned.1.call-update) | async-done | bytes 4718608 | tf_op jit(solution)/shard_map/all_gather | solution.py:81
  173.9 9.5 %gather_fusion.1 = bf16[40,36864]{1,0:T(8,128)(2,1)} fusion(bf16[64,36864]{1,0:T(8,128)(2,1)} %bitcast.89, s32[1024]{0:T(1024)} %pad_clamp_fusion), kind=kCustom, calls=%fused_computation.1 | custom fusion | bytes 5898400 | tf_op jit(solution)/shard_map/jit(_take)/gather | solution.py:81
  183.4 5.6 %gather.15 = bf16[2560,576]{1,0:T(8,128)(2,1)S(1)} reshape(bf16[40,36864]{1,0:T(8,128)(2,1)} %gather_fusion.1) | data formatting | bytes 5898240 | tf_op jit(solution)/shard_map/jit(_take)/gather | solution.py:81
  189.0 2.5 broadcast_select_fusion
  191.6 4.8 %copy.62 = bf16[2560,576]{0,1:T(8,128)(2,1)} copy(bf16[2560,576]{1,0:T(8,128)(2,1)} %broadcast_select_fusion) | data formatting | bytes 5898240
  196.4 64.5 %while.15 = (s32[]{:T(128)}, f32[64,32]{0,1:T(8,128)S(1)}, f32[64,32]{0,1:T(8,128)S(1)}, f32[64,32,512]{2,1,0:T(8,128)}, s32[5]{0:T(128)S(1)}, /*index=5*/s32[]{...) while((s32[]{:T(128)}, f32[64,32]{0,1:T(8,128)S(1)}, ...), condition=%wide.region_3.4_spmd.clone, body=%wide.region_0.3_spmd.clone.sunk | while | flops 2294295552 | bytes 24848084 | solution.py:51
  197.9 3.9 %bitcast_reduce_fusion.2 = (f32[64,32]{0,1:T(8,128)S(1)}, f32[512,64,32]{0,1,2:T(8,128)S(1)}) fusion(pred[512]{0:T(512)(128)(4,1)S(1)} %add_compare_fusion.2, bf16[64,32,576]{2,0,1:T(8,128)(2,1)} %get-tuple-element.218, bf16[2560,576]{0,1:T(8,128)(2,1)} %get-tuple-element.217, s32[]{:T(128)S(6)} %select_n.128), kind=kOutput, calls=%fused_computation.3.clone.1 | convolution fusion | flops 1211103232 | bytes 7414276 | tf_op jit(solution)/shard_map/while/body/eval_jaxpr/qhc,kc->qhk/dot_general | solution.py:18
  201.8 1.4 fusion.52
  203.3 5.1 %fusion.54 = f32[64,32,512]{2,1,0:T(8,128)} fusion(f32[64,32,512]{2,1,0:T(8,128)} %get-tuple-element.202, bf16[64,32,512]{2,0,1:T(8,128)(2,1)S(1)} %get-tuple-element.185, f32[64,32]{1,0:T(8,128)S(1)} %copy.87, pred[]{:T(512)S(6)} %compare.3, bf16[2560,576]{0,1:T(8,128)(2,1)} %get-tuple-element.217, s32[]{:T(128)S(6)} %select_n.128), kind=kOutput, calls=%fused_computation.7.clone.1 | convolution fusion | flops 1076887552 | bytes 11018245 | tf_op jit(solution)/shard_map/while/body/eval_jaxpr/qhk,kc->qhc/dot_general | solution.py:26
  209.7 3.9 %bitcast_reduce_fusion.2 = (f32[64,32]{0,1:T(8,128)S(1)}, f32[512,64,32]{0,1,2:T(8,128)S(1)}) fusion(pred[512]{0:T(512)(128)(4,1)S(1)} %add_compare_fusion.2, bf16[64,32,576]{2,0,1:T(8,128)(2,1)} %get-tuple-element.218, bf16[2560,576]{0,1:T(8,128)(2,1)} %get-tuple-element.217, s32[]{:T(128)S(6)} %select_n.128), kind=kOutput, calls=%fused_computation.3.clone.1 | convolution fusion | flops 1211103232 | bytes 7414276 | tf_op jit(solution)/shard_map/while/body/eval_jaxpr/qhc,kc->qhk/dot_general | solution.py:18
  213.6 1.4 fusion.52
  215.1 6.4 %fusion.54 = f32[64,32,512]{2,1,0:T(8,128)} fusion(f32[64,32,512]{2,1,0:T(8,128)} %get-tuple-element.202, bf16[64,32,512]{2,0,1:T(8,128)(2,1)S(1)} %get-tuple-element.185, f32[64,32]{1,0:T(8,128)S(1)} %copy.87, pred[]{:T(512)S(6)} %compare.3, bf16[2560,576]{0,1:T(8,128)(2,1)} %get-tuple-element.217, s32[]{:T(128)S(6)} %select_n.128), kind=kOutput, calls=%fused_computation.7.clone.1 | convolution fusion | flops 1076887552 | bytes 11018245 | tf_op jit(solution)/shard_map/while/body/eval_jaxpr/qhk,kc->qhc/dot_general | solution.py:26
  222.8 3.9 %bitcast_reduce_fusion.2 = (f32[64,32]{0,1:T(8,128)S(1)}, f32[512,64,32]{0,1,2:T(8,128)S(1)}) fusion(pred[512]{0:T(512)(128)(4,1)S(1)} %add_compare_fusion.2, bf16[64,32,576]{2,0,1:T(8,128)(2,1)} %get-tuple-element.218, bf16[2560,576]{0,1:T(8,128)(2,1)} %get-tuple-element.217, s32[]{:T(128)S(6)} %select_n.128), kind=kOutput, calls=%fused_computation.3.clone.1 | convolution fusion | flops 1211103232 | bytes 7414276 | tf_op jit(solution)/shard_map/while/body/eval_jaxpr/qhc,kc->qhk/dot_general | solution.py:18
  226.7 1.4 fusion.52
  228.2 6.4 %fusion.54 = f32[64,32,512]{2,1,0:T(8,128)} fusion(f32[64,32,512]{2,1,0:T(8,128)} %get-tuple-element.202, bf16[64,32,512]{2,0,1:T(8,128)(2,1)S(1)} %get-tuple-element.185, f32[64,32]{1,0:T(8,128)S(1)} %copy.87, pred[]{:T(512)S(6)} %compare.3, bf16[2560,576]{0,1:T(8,128)(2,1)} %get-tuple-element.217, s32[]{:T(128)S(6)} %select_n.128), kind=kOutput, calls=%fused_computation.7.clone.1 | convolution fusion | flops 1076887552 | bytes 11018245 | tf_op jit(solution)/shard_map/while/body/eval_jaxpr/qhk,kc->qhc/dot_general | solution.py:26
  235.9 3.9 %bitcast_reduce_fusion.2 = (f32[64,32]{0,1:T(8,128)S(1)}, f32[512,64,32]{0,1,2:T(8,128)S(1)}) fusion(pred[512]{0:T(512)(128)(4,1)S(1)} %add_compare_fusion.2, bf16[64,32,576]{2,0,1:T(8,128)(2,1)} %get-tuple-element.218, bf16[2560,576]{0,1:T(8,128)(2,1)} %get-tuple-element.217, s32[]{:T(128)S(6)} %select_n.128), kind=kOutput, calls=%fused_computation.3.clone.1 | convolution fusion | flops 1211103232 | bytes 7414276 | tf_op jit(solution)/shard_map/while/body/eval_jaxpr/qhc,kc->qhk/dot_general | solution.py:18
  239.8 1.4 fusion.52
  241.3 6.4 %fusion.54 = f32[64,32,512]{2,1,0:T(8,128)} fusion(f32[64,32,512]{2,1,0:T(8,128)} %get-tuple-element.202, bf16[64,32,512]{2,0,1:T(8,128)(2,1)S(1)} %get-tuple-element.185, f32[64,32]{1,0:T(8,128)S(1)} %copy.87, pred[]{:T(512)S(6)} %compare.3, bf16[2560,576]{0,1:T(8,128)(2,1)} %get-tuple-element.217, s32[]{:T(128)S(6)} %select_n.128), kind=kOutput, calls=%fused_computation.7.clone.1 | convolution fusion | flops 1076887552 | bytes 11018245 | tf_op jit(solution)/shard_map/while/body/eval_jaxpr/qhk,kc->qhc/dot_general | solution.py:26
  249.0 3.9 %bitcast_reduce_fusion.2 = (f32[64,32]{0,1:T(8,128)S(1)}, f32[512,64,32]{0,1,2:T(8,128)S(1)}) fusion(pred[512]{0:T(512)(128)(4,1)S(1)} %add_compare_fusion.2, bf16[64,32,576]{2,0,1:T(8,128)(2,1)} %get-tuple-element.218, bf16[2560,576]{0,1:T(8,128)(2,1)} %get-tuple-element.217, s32[]{:T(128)S(6)} %select_n.128), kind=kOutput, calls=%fused_computation.3.clone.1 | convolution fusion | flops 1211103232 | bytes 7414276 | tf_op jit(solution)/shard_map/while/body/eval_jaxpr/qhc,kc->qhk/dot_general | solution.py:18
  252.9 1.4 fusion.52
  254.4 6.4 %fusion.54 = f32[64,32,512]{2,1,0:T(8,128)} fusion(f32[64,32,512]{2,1,0:T(8,128)} %get-tuple-element.202, bf16[64,32,512]{2,0,1:T(8,128)(2,1)S(1)} %get-tuple-element.185, f32[64,32]{1,0:T(8,128)S(1)} %copy.87, pred[]{:T(512)S(6)} %compare.3, bf16[2560,576]{0,1:T(8,128)(2,1)} %get-tuple-element.217, s32[]{:T(128)S(6)} %select_n.128), kind=kOutput, calls=%fused_computation.7.clone.1 | convolution fusion | flops 1076887552 | bytes 11018245 | tf_op jit(solution)/shard_map/while/body/eval_jaxpr/qhk,kc->qhc/dot_general | solution.py:26
  261.8 2.9 %divide_convert_fusion = bf16[64,32,512]{2,1,0:T(8,128)(2,1)S(1)} fusion(f32[64,32,512]{2,1,0:T(8,128)} %get-tuple-element.46, f32[64,32]{1,0:T(8,128)S(1)} %get-tuple-element.118, f32[64,32]{1,0:T(8,128)S(1)} %get-tuple-element.119, f32[64,32,64]{2,1,0:T(8,128)S(1)} %copy-done.3, f32[64,32]{1,0:T(8,128)S(1)} %max.6, pred[64,64]{1,0:T(8,128)(4,1)S(1)} %copy-done.13, ...), kind=kOutput, calls=%fused_computation.23 | convolution fusion | flops 138805248 | bytes 7512064 | tf_op jit(solution)/shard_map/qhk,kc->qhc/dot_general | solution.py:26
  264.7 2.6 copy.78
  (107 shorter events, 11.8 us)
Async XLA Ops:
  7.2 108.1 %copy-start = (bf16[1,512,1792]{2,1,0:T(8,128)(2,1)S(1)}, bf16[1,512,1792]{2,1,0:T(8,128)(2,1)}, u32[]{:S(2)}) copy-start(bf16[1,512,1792]{2,1,0:T(8,128)(2,1)} %param.25) | copy-start | bytes 5505028
  7.2 20.8 %copy-start.18 = (s32[1,64]{1,0:T(1,128)S(1)}, s32[1,64]{1,0:T(1,128)}, u32[]{:S(2)}) copy-start(s32[1,64]{1,0:T(1,128)} %param.15) | copy-start | bytes 772
  7.2 20.8 %copy-start.2 = (bf16[64,9216]{1,0:T(8,128)(2,1)S(1)}, bf16[64,9216]{1,0:T(8,128)(2,1)}, u32[]{:S(2)}) copy-start(bf16[64,9216]{1,0:T(8,128)(2,1)} %param.14) | copy-start | bytes 3538948
  8.9 0.6 copy-start.14
  9.5 0.6 copy-start.5
  14.7 39.0 %all-to-all-start.1 = ((bf16[64,4,1792]{2,1,0:T(4,128)(2,1)}), bf16[64,4,1792]{2,1,0:T(4,128)(2,1)}, u32[]{:S(2)}, u32[]{:S(2)}) async-start(bf16[64,4,1792]{2,1,0:T(4,128)(2,1)} %bitcast.90), calls=%async_computation.1 | async-start | bytes 1835008 | tf_op jit(solution)/shard_map/all_to_all | solution.py:102
  53.7 37.6 %all-to-all-start = ((bf16[64,2,4608]{2,1,0:T(2,128)(2,1)}), bf16[64,2,4608]{2,1,0:T(2,128)(2,1)S(1)}, u32[]{:S(2)}, u32[]{:S(2)}) async-start(bf16[64,2,4608]{2,1,0:T(2,128)(2,1)} %reshape.188), calls=%async_computation | async-start | bytes 2359296 | tf_op jit(solution)/shard_map/all_to_all | solution.py:76
  59.9 54.0 %all-reduce.2.cloned.1.call-start = ((), (), s32[]{:S(2)}) async-start(), calls=%async_computation.3 | async-start | bytes 1048576 | tf_op jit(solution)/shard_map/psum | solution.py:107
  66.6 107.3 %all-gather.3.cloned.1.call-start = ((), (), s32[]{:S(2)}) async-start(), calls=%async_computation.4 | async-start | bytes 5898240 | tf_op jit(solution)/shard_map/all_gather | solution.py:81
  115.3 15.5 %copy-start.19 = (s32[1,40]{1,0:T(1,128)S(1)}, s32[1,40]{1,0:T(1,128)}, u32[]{:S(2)}) copy-start(s32[1,40]{1,0:T(1,128)} %param.16) | copy-start | bytes 484
  115.3 16.3 %copy-start.17 = (f32[64,8]{0,1:T(8,128)S(1)}, f32[64,8]{0,1:T(8,128)}, u32[]{:S(2)}) copy-start(f32[64,8]{0,1:T(8,128)} %param.23) | copy-start | bytes 6148
  117.6 38.3 %all-to-all-start.2 = ((bf16[64,4,1792]{2,1,0:T(4,128)(2,1)}), bf16[64,4,1792]{2,1,0:T(4,128)(2,1)S(1)}, u32[]{:S(2)}, u32[]{:S(2)}) async-start(bf16[64,4,1792]{2,1,0:T(4,128)(2,1)} %copy.71), calls=%async_computation.2 | async-start | bytes 1835008 | tf_op jit(solution)/shard_map/all_to_all | solution.py:110
  136.8 2.5 copy-start.20
  136.8 3.1 %copy-start.6 = (s32[64,8]{1,0:T(8,128)S(1)}, s32[64,8]{1,0:T(8,128)}, u32[]{:S(2)}) copy-start(s32[64,8]{1,0:T(8,128)} %copy-done.5) | copy-start | bytes 6148
  136.8 3.1 %copy-start.8 = (f32[64,8]{1,0:T(8,128)S(1)}, f32[64,8]{1,0:T(8,128)}, u32[]{:S(2)}) copy-start(f32[64,8]{1,0:T(8,128)} %copy.69) | copy-start | bytes 6148
  136.8 3.1 %copy-start.15 = (pred[64,8]{1,0:T(8,128)(4,1)S(1)}, pred[64,8]{1,0:T(8,128)(4,1)}, u32[]{:S(2)}) copy-start(pred[64,8]{1,0:T(8,128)(4,1)} %copy-done.14) | copy-start | bytes 1540
  136.8 4.0 %copy-start.10 = (bf16[64,576]{1,0:T(8,128)(2,1)S(1)}, bf16[64,576]{1,0:T(8,128)(2,1)}, u32[]{:S(2)}) copy-start(bf16[64,576]{1,0:T(8,128)(2,1)} %param.19) | copy-start | bytes 221188
  139.9 0.9 copy-start.12
  155.8 0.8 copy-start.7
  183.4 5.6 %copy-start.16 = (pred[2560]{0:T(1024)(128)(4,1)S(1)}, pred[2560]{0:T(1024)(128)(4,1)}, u32[]{:S(2)}) copy-start(pred[2560]{0:T(1024)(128)(4,1)} %broadcast_in_dim.109) | copy-start | bytes 7684
  191.6 4.8 %copy-start.4 = (f32[64,32]{0,1:T(8,128)S(1)}, f32[64,32]{0,1:T(8,128)}, u32[]{:S(2)}) copy-start(f32[64,32]{0,1:T(8,128)} %custom-call.1) | copy-start | bytes 24580
  196.4 64.6 %copy-start.9 = (f32[64,32]{1,0:T(8,128)S(1)}, f32[64,32]{1,0:T(8,128)}, u32[]{:S(2)}) copy-start(f32[64,32]{1,0:T(8,128)} %get-tuple-element.124) | copy-start | bytes 24580
  196.4 64.7 %copy-start.3 = (f32[64,32,64]{2,1,0:T(8,128)S(1)}, f32[64,32,64]{2,1,0:T(8,128)}, u32[]{:S(2)}) copy-start(f32[64,32,64]{2,1,0:T(8,128)} %get-tuple-element.125) | copy-start | bytes 1572868
  196.4 64.7 %copy-start.13 = (pred[64,64]{1,0:T(8,128)(4,1)S(1)}, pred[64,64]{1,0:T(8,128)(4,1)}, u32[]{:S(2)}) copy-start(pred[64,64]{1,0:T(8,128)(4,1)} %copy-done.12) | copy-start | bytes 12292
  196.4 65.3 %copy-start.11 = (bf16[64,576]{1,0:T(8,128)(2,1)S(1)}, bf16[64,576]{1,0:T(8,128)(2,1)}, u32[]{:S(2)}) copy-start(bf16[64,576]{1,0:T(8,128)(2,1)} %param.19) | copy-start | bytes 221188
  261.8 5.5 %copy-start.1 = (bf16[1,512,1792]{2,1,0:T(8,128)(2,1)S(1)}, bf16[1,512,1792]{2,1,0:T(8,128)(2,1)}, u32[]{:S(2)}) copy-start(bf16[1,512,1792]{2,1,0:T(8,128)(2,1)} %param.25) | copy-start | bytes 5505028
Sparse Core Ops, SparseCore 0:
  66.7 47.0 all-reduce.1
  116.2 57.5 all-gather.2
where the time goes:
time: 275 us; the launch traced here: 274 us
  waiting for transfers between devices  86 us (31%)
  matrix products  62.9 us (23%)
  local copies, waits for them, and re-layouts  55.3 us (20%)
  starting transfers between devices  32.1 us (12%)
  other arithmetic  18.9 us (7%)
  between operations  15.1 us (5%)
  loops' own time  3.73 us (1%)
    dot_general x6, matrix products, absorb_block(): jnp.einsum('qhk,kc->qhc', weights.astype(jnp.bfloat16), key_rows[:, :late...  33.8 us
    all_to_all x1, waiting for transfers between devices, body(): lax.all_to_all(ordered.reshape(groups, -1, row_width), 'dp', split_axis=0...  24.6 us
    dot_general x6, matrix products, absorb_block(): jnp.einsum('qhc,kc->qhk', local_queries, key_rows, preferred_element_type...  21.9 us
    unnamed x48, local copies, waits for them, and re-layouts  18.1 us
    all_to_all x1, waiting for transfers between devices, body(): lax.all_to_all(paired, 'dp', split_axis=0, concat_axis=0, tiled=True)  16.4 us
    all_gather x1, waiting for transfers between devices, body(): lax.all_gather(arrived, 'mp', axis=1, tiled=True)  16.3 us
    psum x1, waiting for transfers between devices, body(): preacts = lax.psum(preacts.astype(jnp.bfloat16), 'mp').astype(jnp.float32)  16.1 us
    gather x2, local copies, waits for them, and re-layouts, body(): jnp.take(lax.all_gather(arrived, 'mp', axis=1, tiled=True), source, axis=0)  15.1 us
  transfers between devices with their start and end apart: 5, of which 5 were waited for; matrix products, arithmetic and copies ran while one was open for 15% of the time, Pallas kernels for 0%

commit v1 on v0

v1 whole, which is shorter than its diff:
```python
import functools

import jax
import jax.numpy as jnp
from jax import lax
from jax.experimental import pallas as pl
from jax.experimental.pallas import tpu as pltpu
from jax.sharding import PartitionSpec as P

MESH = pl.DeviceIdType.MESH
BF = jnp.bfloat16
F32 = jnp.float32
I32 = jnp.int32

KVL = 512
ENT = 576
PAGE = 64
CAP = 4
CHIPS = 32
HALF = 896
CHUNKS = 5
KEYS = 256
WIDE = 1152
HEADS = 32
ROWS = 2048
BLK = 512
LOW = -1e30
GAIN = 192 ** (-0.5) * 1.4426950408889634
FIRST = 16
STEP = 4


def dot(a, b):
    return jnp.dot(a, b, preferred_element_type=F32)


def dot_nt(a, b):
    return lax.dot_general(a, b, (((1,), (1,)), ((), ())), preferred_element_type=F32)


def iota(shape, axis):
    return lax.broadcasted_iota(I32, shape, axis)


def kernel(
    pool_h, slots_s, source_v, pages_s, queries_h, suffix_v, hidden_v, ids_v, exp_slots_v, gates_v, wgu_h, wdn_h,
    context_h, moe_v,
    pool, tmp_lat, tmp_rope, send_p, arr, fwd, work, keys, q_a, q_b, suf_k, acc, peak, total, out, q_raw,
    wgu, wdn, disp, got, part, rsb, hid, pf, pxs, pxr, ret_s, ret_r, mixw, order_v, order_s,
    ld, disp_ss, disp_rs, page_ss, page_rs, fwd_ss, fwd_rs, sib_ss, sib_rs, x_ss, x_rs, ret_ss, ret_rs, ag_ss, ag_rs,
):
    dp = lax.axis_index("dp")
    mp = lax.axis_index("mp")
    core = lax.rem(dp, 2)
    chip = dp // 2
    y = chip // 8
    z = lax.rem(chip, 8)
    other = 1 - core
    sibling = (chip * 2 + other, mp)

    def shift(k):
        dz = lax.rem(3 * k, 8)
        dy = lax.rem(k // 8 + k, 4)
        return dy, dz

    def to_chip(k):
        dy, dz = shift(k)
        return lax.rem(y + dy, 4) * 8 + lax.rem(z + dz, 8)

    def from_chip(k):
        dy, dz = shift(k)
        return lax.rem(y + 4 - dy, 4) * 8 + lax.rem(z + 8 - dz, 8)

    def x_peer(step):
        return (dp, lax.rem(mp + step, 4))

    barrier = pltpu.get_barrier_semaphore()

    def greet(k, carry):
        pl.semaphore_signal(barrier, inc=1, device_id=(to_chip(k) * 2 + core, mp), device_id_type=MESH)
        return carry

    lax.fori_loop(1, CHIPS, greet, 0)
    pl.semaphore_signal(barrier, inc=1, device_id=sibling, device_id_type=MESH)
    for step in (1, 2, 3):
        pl.semaphore_signal(barrier, inc=1, device_id=x_peer(step), device_id_type=MESH)

    load_pool = pltpu.make_async_copy(pool_h, pool, ld.at[0])
    load_pool.start()
    load_q = pltpu.make_async_copy(queries_h, q_raw, ld.at[1])
    load_q.start()
    load_gu = pltpu.make_async_copy(wgu_h.at[0], wgu, ld.at[2])
    load_gu.start()
    load_dn = pltpu.make_async_copy(wdn_h.at[0], wdn, ld.at[3])
    load_dn.start()

    src = source_v[...]
    src_y = src // 16
    src_z = lax.rem(src // 2, 8)
    res = lax.rem(3 * lax.rem(z + 8 - src_z, 8), 8)
    lap = lax.rem(lax.rem(y + 4 - src_y, 4) + 8 - res, 4)
    lane40 = iota((1, 40), 1)
    rank_key = (lap * 8 + res) * 64 + lane40
    sub = iota((40, 40), 0)
    lane = iota((40, 40), 1)
    key_rows = jnp.broadcast_to(rank_key, (40, 40))
    key_cols = jnp.sum(jnp.where(sub == lane, key_rows, 0), axis=1, keepdims=True)
    rank_col = jnp.sum(jnp.where(key_rows < key_cols, 1, 0), axis=1, keepdims=True)
    src_col = jnp.sum(jnp.where(sub == lane, jnp.broadcast_to(src, (40, 40)), 0), axis=1, keepdims=True)
    hit = iota((40, 128), 1) == rank_col
    seen_col = jnp.where(iota((40, 128), 0) < pages_s[0], 1, 0)
    ordered = jnp.sum(jnp.where(hit, src_col, 0), axis=0, keepdims=True)
    seen = jnp.sum(jnp.where(hit, seen_col, 0), axis=0, keepdims=True)
    row8 = iota((8, 128), 0)
    order_v[...] = jnp.where(row8 == 0, ordered, jnp.where(row8 == 1, seen, 0))
    order_copy = pltpu.make_async_copy(order_v, order_s, ld.at[4])
    order_copy.start()

    ids = ids_v[...]
    exp_slots = exp_slots_v[...]
    target = jnp.where((exp_slots >= 0) & (ids < CHIPS), ids * CAP + exp_slots, -1)
    half_lane = iota((8, 128), 1) // 64
    target = jnp.concatenate([target, target], axis=1)
    target = jnp.where(target >= 0, target * 2 + half_lane, -1)
    gates = jnp.concatenate([gates_v[...], gates_v[...]], axis=1)
    row = iota((256, 128), 0)
    wanted = ((row // 8) * 4 + lax.rem(row, 4)) * 2 + lax.rem(row // 4, 2)
    select = jnp.zeros((256, 128), F32)
    mix = jnp.zeros((256, 128), F32)
    for k in range(8):
        match = wanted == target[k : k + 1, :]
        select = select + jnp.where(match, 1.0, 0.0)
        mix = mix + jnp.where(match, gates[k : k + 1, :], 0.0)
    mixw[...] = mix
    hidden = hidden_v[...]
    halves = jnp.concatenate([hidden[:, :HALF], hidden[:, HALF:]], axis=0)
    picked = dot(select.astype(BF), halves)
    disp[...] = picked.reshape(CHIPS, 8, HALF).astype(BF)

    pl.semaphore_wait(barrier, CHIPS + 3)

    def disp_copy(k, q):
        return pltpu.make_async_remote_copy(
            src_ref=disp.at[q], dst_ref=got.at[core, chip], send_sem=disp_ss.at[k], recv_sem=disp_rs.at[k],
            device_id=(q * 2 + core, mp), device_id_type=MESH,
        )

    def disp_start(k, carry):
        disp_copy(k, to_chip(k)).start()
        return carry

    lax.fori_loop(1, CHIPS, disp_start, 0)
    got[core, chip] = disp[chip]

    load_pool.wait()
    perm_row = iota((256, 256), 0)
    perm_col = iota((256, 256), 1)
    perm = jnp.where((lax.rem(perm_row, 16) == perm_col // 16) & (perm_row // 16 == lax.rem(perm_col, 16)), 1.0, 0.0).astype(BF)
    for g in range(4):
        lat_rows = []
        rope_rows = []
        for t in range(16):
            start = t * ENT
            lat_rows.append(pool[g * 16 : g * 16 + 16, start : start + KVL])
            rope = pool[g * 16 : g * 16 + 16, start + KVL : start + ENT]
            rope_rows.append(jnp.concatenate([rope, rope], axis=1))
        lat = dot(perm, jnp.concatenate(lat_rows, axis=0)).astype(BF)
        rope = dot(perm, jnp.concatenate(rope_rows, axis=0)).astype(BF)
        for p in range(16):
            for c in range(4):
                tmp_lat[g * 16 + p, c * 16 : c * 16 + 16, :] = lat[p * 16 : p * 16 + 16, c * 128 : c * 128 + 128]
            tmp_rope[g * 16 + p] = rope[p * 16 : p * 16 + 16, :]

    low_lane = iota((16, 128), 1) < 64

    def page_copy(k, q):
        return pltpu.make_async_remote_copy(
            src_ref=send_p.at[q], dst_ref=arr.at[chip], send_sem=page_ss.at[k], recv_sem=page_rs.at[k],
            device_id=(q * 2 + core, mp), device_id_type=MESH,
        )

    def page_fill(q):
        first = slots_s[0, 2 * q]
        second = slots_s[0, 2 * q + 1]
        send_p[q, 0:64, :] = tmp_lat[first]
        send_p[q, 64:80, :] = jnp.where(low_lane, tmp_rope[first], tmp_rope[second])
        send_p[q, 80:144, :] = tmp_lat[second]

    def page_start(k, carry):
        q = to_chip(k)
        page_fill(q)
        page_copy(k, q).start()
        return carry

    lax.fori_loop(1, CHIPS, page_start, 0)
    page_fill(chip)
    arr[chip] = send_p[chip]

    load_q.wait()
    zeros = jnp.zeros((64, 64), BF)
    for h in range(HEADS):
        rows = slice(h * 64, h * 64 + 64)
        start = h * ENT
        lat = q_raw[:, start : start + KVL]
        rope = q_raw[:, start + KVL : start + ENT]
        q_a[rows, 0:KVL] = lat
        q_a[rows, KVL : KVL + 128] = jnp.concatenate([rope, zeros], axis=1)
        q_b[rows, 0:128] = jnp.concatenate([zeros, rope], axis=1)
        q_b[rows, 128 : 128 + KVL] = lat

    suf_k[:, 0:KVL] = suffix_v[:, 0:KVL]
    suf_k[:, KVL : KVL + 128] = jnp.concatenate([suffix_v[:, KVL:ENT], zeros], axis=1)

    def suffix_block(b, carry):
        rows = pl.ds(pl.multiple_of(b * BLK, BLK), BLK)
        s = dot_nt(q_a[rows, :], suf_k[...]) * GAIN
        token = lax.rem(iota((BLK, 64), 0), 64)
        s = jnp.where(iota((BLK, 64), 1) <= token, s, LOW)
        top = jnp.max(s, axis=1, keepdims=True)
        w = jnp.exp2(s - top)
        peak[rows, :] = jnp.broadcast_to(top, (BLK, 128))
        total[rows, :] = jnp.concatenate([w, jnp.zeros((BLK, 64), F32)], axis=1)
        acc[rows, :] = dot(w.astype(BF), suf_k[:, 0:KVL])
        return carry

    lax.fori_loop(0, ROWS // BLK, suffix_block, 0)

    def forward_copy(k, q):
        return pltpu.make_async_remote_copy(
            src_ref=arr.at[q, pl.ds(pl.multiple_of(64 * other, 16), 80)], dst_ref=fwd.at[q],
            send_sem=fwd_ss.at[k], recv_sem=fwd_rs.at[k], device_id=sibling, device_id_type=MESH,
        )

    def arrive(k, carry):
        q = from_chip(k)
        page_copy(k, q).wait_recv()
        forward_copy(k, q).start()
        return carry

    def arrivals(stage):
        if stage == 0:
            forward_copy(0, chip).start()
            lax.fori_loop(1, FIRST, arrive, 0)
        else:
            lax.fori_loop(FIRST + STEP * (stage - 1), FIRST + STEP * stage, arrive, 0)

    def both_halves(tile):
        wide = tile.astype(F32)
        turned = pltpu.roll(wide, 64, 1)
        keep = (iota((16, 128), 1) // 64) == core
        return jnp.where(keep, wide, turned).astype(BF)

    def settle(k, carry):
        q = from_chip(k)
        forward_copy(k, q).wait_recv()
        work[0, q, 0:64, :] = arr[q, pl.ds(pl.multiple_of(80 * core, 16), 64), :]
        work[0, q, 64:80, :] = both_halves(arr[q, 64:80, :])
        work[1, q, 0:64, :] = fwd[q, pl.ds(pl.multiple_of(16 * core, 16), 64), :]
        work[1, q, 64:80, :] = both_halves(fwd[q, pl.ds(pl.multiple_of(64 * other, 16), 16), :])
        return carry

    mine = pl.ds(pl.multiple_of(mp * 64, 64), 64)

    def near_copy(ch, step):
        way = 0 if step == 1 else 1
        return pltpu.make_async_remote_copy(
            src_ref=keys.at[ch, mine], dst_ref=keys.at[ch, mine], send_sem=ag_ss.at[ch, way], recv_sem=ag_rs.at[ch, way],
            device_id=x_peer(step), device_id_type=MESH,
        )

    def far_copy(ch, step):
        way = 2 if step == 1 else 3
        owner = lax.rem(mp + 4 - step, 4)
        begin = owner * 64 + (0 if step == 1 else 32)
        rows = pl.ds(pl.multiple_of(begin, 32), 32)
        return pltpu.make_async_remote_copy(
            src_ref=keys.at[ch, rows], dst_ref=keys.at[ch, rows], send_sem=ag_ss.at[ch, way], recv_sem=ag_rs.at[ch, way],
            device_id=x_peer(step), device_id_type=MESH,
        )

    def gather_chunk(ch):
        if ch == 0:
            lax.fori_loop(0, FIRST, settle, 0)
        else:
            lax.fori_loop(FIRST + STEP * (ch - 1), FIRST + STEP * ch, settle, 0)

        def pick(i, carry):
            a = jnp.clip(order_s[0, ch * 8 + i], 0, 63)
            b = jnp.clip(order_s[0, ch * 8 + 4 + i], 0, 63)
            rel_a = lax.rem(lax.rem(a, 2) + core, 2)
            rel_b = lax.rem(lax.rem(b, 2) + core, 2)
            page_a = work[rel_a, a // 2]
            page_b = work[rel_b, b // 2]
            rows = pl.ds(pl.multiple_of(mp * 64 + i * 16, 16), 16)
            for c in range(4):
                keys[ch, rows, c * 128 : c * 128 + 128] = page_a[c * 16 : c * 16 + 16, :]
                keys[ch, rows, 640 + c * 128 : 640 + c * 128 + 128] = page_b[c * 16 : c * 16 + 16, :]
            keys[ch, rows, 512:640] = jnp.where(low_lane, page_a[64:80, :], page_b[64:80, :])
            return carry

        lax.fori_loop(0, 4, pick, 0)
        near_copy(ch, 1).start()
        near_copy(ch, 3).start()

    def relay_chunk(ch):
        near_copy(ch, 1).wait_recv()
        far_copy(ch, 1).start()
        near_copy(ch, 3).wait_recv()
        far_copy(ch, 3).start()

    def attend_chunk(ch):
        far_copy(ch, 1).wait_recv()
        far_copy(ch, 3).wait_recv()
        page_lane = lax.rem(iota((1, KEYS), 1) // 16, 4)

        def bias(base):
            value = jnp.zeros((1, KEYS), F32)
            for i in range(4):
                shown = order_s[1, ch * 8 + base + i].astype(F32)
                value = jnp.where(page_lane == i, (shown - 1.0) * -LOW, value)
            return value

        bias_a = bias(0)
        bias_b = bias(4)

        def block(b, carry):
            rows = pl.ds(pl.multiple_of(b * BLK, BLK), BLK)
            s_a = dot_nt(q_a[rows, :], keys[ch, :, 0:640]) * GAIN + bias_a
            s_b = dot_nt(q_b[rows, :], keys[ch, :, 512:1152]) * GAIN + bias_b
            old = peak[rows, 0:1]
            top = jnp.maximum(jnp.max(jnp.maximum(s_a, s_b), axis=1, keepdims=True), old)
            factor = jnp.exp2(old - top)
            w_a = jnp.exp2(s_a - top)
            w_b = jnp.exp2(s_b - top)
            both = w_a + w_b
            peak[rows, :] = jnp.broadcast_to(top, (BLK, 128))
            total[rows, :] = total[rows, :] * factor + both[:, 0:128] + both[:, 128:256]
            acc[rows, :] = (
                acc[rows, :] * factor
                + dot(w_a.astype(BF), keys[ch, :, 0:KVL])
                + dot(w_b.astype(BF), keys[ch, :, 640 : 640 + KVL])
            )
            return carry

        lax.fori_loop(0, ROWS // BLK, block, 0)

    def disp_wait(k, carry):
        disp_copy(k, to_chip(k)).wait_recv()
        return carry

    lax.fori_loop(1, CHIPS, disp_wait, 0)
    got_copy = pltpu.make_async_remote_copy(
        src_ref=got.at[core], dst_ref=got.at[core], send_sem=sib_ss.at[0], recv_sem=sib_rs.at[0],
        device_id=sibling, device_id_type=MESH,
    )
    got_copy.start()
    load_gu.wait()
    got_copy.wait_recv()
    rows512 = got[...].astype(F32).reshape(512, HALF).astype(BF)
    pr = iota((256, 512), 0)
    pc = iota((256, 512), 1)
    same = (pr // 4 == pc // 8) & (lax.rem(pr, 4) == lax.rem(pc, 4))
    left = dot(jnp.where(same & (lax.rem(pc // 4, 2) == 0), 1.0, 0.0).astype(BF), rows512).astype(BF)
    right = dot(jnp.where(same & (lax.rem(pc // 4, 2) == 1), 1.0, 0.0).astype(BF), rows512).astype(BF)
    part[...] = (dot(left, wgu[0:HALF, :]) + dot(right, wgu[HALF : 2 * HALF, :])).astype(BF)

    def sum_copy(step):
        there = lax.rem(mp + step, 4)
        return pltpu.make_async_remote_copy(
            src_ref=part.at[pl.ds(pl.multiple_of(there * 64, 64), 64)], dst_ref=rsb.at[mp],
            send_sem=x_ss.at[step - 1], recv_sem=x_rs.at[step - 1], device_id=x_peer(step), device_id_type=MESH,
        )

    for step in (2, 1, 3):
        sum_copy(step).start()
    rsb[mp] = part[mine, :]

    arrivals(0)

    for step in (1, 2, 3):
        sum_copy(step).wait_recv()
    pre = rsb[0].astype(F32) + rsb[1].astype(F32) + rsb[2].astype(F32) + rsb[3].astype(F32)
    gate = pre[:, 0:512]
    hid[mine, :] = (gate / (1.0 + jnp.exp(-gate)) * pre[:, 512:1024]).astype(BF)

    def hid_copy(step):
        return pltpu.make_async_remote_copy(
            src_ref=hid.at[mine], dst_ref=hid.at[mine],
            send_sem=x_ss.at[step + 2], recv_sem=x_rs.at[step + 2], device_id=x_peer(step), device_id_type=MESH,
        )

    for step in (2, 1, 3):
        hid_copy(step).start()

    order_copy.wait()
    gather_chunk(0)

    for step in (1, 2, 3):
        hid_copy(step).wait_recv()
    load_dn.wait()
    dr = iota((512, 256), 0)
    dc = iota((512, 256), 1)
    twice = jnp.where((dr // 8 == dc // 4) & (lax.rem(dr, 4) == lax.rem(dc, 4)), 1.0, 0.0).astype(BF)
    doubled = dot(twice, hid[...]).astype(BF)
    is_left = lax.rem(iota((512, HALF), 0) // 4, 2) == 0
    pf[...] = jnp.where(is_left, dot(doubled, wdn[:, 0:HALF]), dot(doubled, wdn[:, HALF : 2 * HALF])).reshape(2, 256, HALF)
    pxs[...] = pf[other].astype(BF)
    part_copy = pltpu.make_async_remote_copy(
        src_ref=pxs, dst_ref=pxr, send_sem=sib_ss.at[1], recv_sem=sib_rs.at[1], device_id=sibling, device_id_type=MESH,
    )
    part_copy.start()

    arrivals(1)
    part_copy.wait_recv()
    ret_s[...] = (pf[core] + pxr[...].astype(F32)).reshape(CHIPS, 8, HALF).astype(BF)

    def ret_copy(k, q):
        return pltpu.make_async_remote_copy(
            src_ref=ret_s.at[q], dst_ref=ret_r.at[chip], send_sem=ret_ss.at[k], recv_sem=ret_rs.at[k],
            device_id=(q * 2 + core, mp), device_id_type=MESH,
        )

    def ret_start(k, carry):
        ret_copy(k, to_chip(k)).start()
        return carry

    lax.fori_loop(1, CHIPS, ret_start, 0)
    ret_r[chip] = ret_s[chip]

    gather_chunk(1)
    relay_chunk(0)
    arrivals(2)
    gather_chunk(2)
    relay_chunk(1)
    arrivals(3)
    gather_chunk(3)
    attend_chunk(0)
    relay_chunk(2)
    arrivals(4)
    gather_chunk(4)
    attend_chunk(1)
    relay_chunk(3)
    attend_chunk(2)
    relay_chunk(4)
    attend_chunk(3)

    def ret_wait(k, carry):
        ret_copy(k, to_chip(k)).wait_recv()
        return carry

    lax.fori_loop(1, CHIPS, ret_wait, 0)
    rows256 = ret_r[...].astype(F32).reshape(256, HALF).astype(BF)
    weights = mixw[...]
    high = weights.astype(BF)
    low = (weights - high.astype(F32)).astype(BF)
    dims = (((0,), (0,)), ((), ()))
    mixed = lax.dot_general(high, rows256, dims, preferred_element_type=F32) + lax.dot_general(
        low, rows256, dims, preferred_element_type=F32
    )
    moe_v[:, 0:HALF] = mixed[0:64].astype(BF)
    moe_v[:, HALF : 2 * HALF] = mixed[64:128].astype(BF)

    attend_chunk(4)

    for h in range(HEADS):
        rows = slice(h * 64, h * 64 + 64)
        whole = jnp.sum(total[rows, :], axis=1, keepdims=True)
        out[:, h * KVL : h * KVL + KVL] = (acc[rows, :] / whole).astype(BF)
    store = pltpu.make_async_copy(out, context_h, ld.at[5])
    store.start()

    def sent(k, carry):
        disp_copy(k, to_chip(k)).wait_send()
        page_copy(k, to_chip(k)).wait_send()
        forward_copy(k, from_chip(k)).wait_send()
        ret_copy(k, to_chip(k)).wait_send()
        return carry

    lax.fori_loop(1, CHIPS, sent, 0)
    forward_copy(0, chip).wait_send()
    got_copy.wait_send()
    part_copy.wait_send()
    for step in (1, 2, 3):
        sum_copy(step).wait_send()
        hid_copy(step).wait_send()
    for ch in range(CHUNKS):
        for step in (1, 3):
            near_copy(ch, step).wait_send()
            far_copy(ch, step).wait_send()
    store.wait()


def body(
    pool, send_slots, page_source, prefix_pages, queries, suffix_kv, hidden_in,
    expert_ids, expert_slots, gate_weights, w_gate_up, w_down,
):
    any_spec = pl.BlockSpec(memory_space=pl.ANY)
    vmem = pl.BlockSpec(memory_space=pltpu.VMEM)
    smem = pl.BlockSpec(memory_space=pltpu.SMEM)
    dma = pltpu.SemaphoreType.DMA
    scratch = [
        pltpu.VMEM((64, 9216), BF),
        pltpu.VMEM((64, 64, 128), BF),
        pltpu.VMEM((64, 16, 128), BF),
        pltpu.VMEM((CHIPS, 144, 128), BF),
        pltpu.VMEM((CHIPS, 144, 128), BF),
        pltpu.VMEM((CHIPS, 80, 128), BF),
        pltpu.VMEM((2, CHIPS, 80, 128), BF),
        pltpu.VMEM((CHUNKS, KEYS, WIDE), BF),
        pltpu.VMEM((ROWS, 640), BF),
        pltpu.VMEM((ROWS, 640), BF),
        pltpu.VMEM((64, 640), BF),
        pltpu.VMEM((ROWS, KVL), F32),
        pltpu.VMEM((ROWS, 128), F32),
        pltpu.VMEM((ROWS, 128), F32),
        pltpu.VMEM((64, HEADS * KVL), BF),
        pltpu.VMEM((64, HEADS * ENT), BF),
        pltpu.VMEM((2 * HALF, 1024), BF),
        pltpu.VMEM((512, 2 * HALF), BF),
        pltpu.VMEM((CHIPS, 8, HALF), BF),
        pltpu.VMEM((2, CHIPS, 8, HALF), BF),
        pltpu.VMEM((256, 1024), BF),
        pltpu.VMEM((4, 64, 1024), BF),
        pltpu.VMEM((256, 512), BF),
        pltpu.VMEM((2, 256, HALF), F32),
        pltpu.VMEM((256, HALF), BF),
        pltpu.VMEM((256, HALF), BF),
        pltpu.VMEM((CHIPS, 8, HALF), BF),
        pltpu.VMEM((CHIPS, 8, HALF), BF),
        pltpu.VMEM((256, 128), F32),
        pltpu.VMEM((8, 128), I32),
        pltpu.SMEM((8, 128), I32),
        dma((6,)),
        dma((CHIPS,)), dma((CHIPS,)),
        dma((CHIPS,)), dma((CHIPS,)),
        dma((CHIPS,)), dma((CHIPS,)),
        dma((2,)), dma((2,)),
        dma((6,)), dma((6,)),
        dma((CHIPS,)), dma((CHIPS,)),
        dma((CHUNKS, 4)), dma((CHUNKS, 4)),
    ]
    context, moe_out = pl.pallas_call(
        kernel,
        out_shape=(
            jax.ShapeDtypeStruct((64, HEADS * KVL), BF),
            jax.ShapeDtypeStruct((64, 2 * HALF), BF),
        ),
        in_specs=[any_spec, smem, vmem, smem, any_spec, vmem, vmem, vmem, vmem, vmem, any_spec, any_spec],
        out_specs=(any_spec, vmem),
        scratch_shapes=scratch,
        compiler_params=pltpu.CompilerParams(
            collective_id=0, has_side_effects=True, vmem_limit_bytes=56 * 2**20
        ),
        name="prefill",
    )(
        pool, send_slots, page_source, prefix_pages, queries, suffix_kv, hidden_in,
        expert_ids.T, expert_slots.T, gate_weights.T, w_gate_up, w_down,
    )
    return context, moe_out


def solution(mesh):
    return jax.shard_map(
        body,
        mesh=mesh,
        in_specs=(
            P("dp", "mp"),
            P("dp", None),
            P("dp", None),
            P("dp"),
            P("dp", "mp"),
            P("dp", None),
            P("dp", "mp"),
            P("dp", None),
            P("dp", None),
            P("dp", None),
            P("dp", "mp", None),
            P("dp", None, "mp"),
        ),
        out_specs=(P("dp", "mp"), P("dp", "mp")),
        check_vma=False,
    )
```

time: 275 us -> 98.6 us (0.36)
  Pallas kernels: 0 us -> 93.3 us
  waiting for transfers between devices: 86 us -> 0 us
  matrix products: 62.9 us -> 0 us
  local copies, waits for them, and re-layouts: 55.3 us -> 3.78 us
  starting transfers between devices: 32.1 us -> 0 us
  other arithmetic: 18.9 us -> 0 us
  between operations: 15.1 us -> 1.3 us
  loops' own time: 3.73 us -> 0 us
    pallas_call x0 -> x1, Pallas kernels: none -> 93.3 us  [body(): pl.pallas_call(kernel, out_shape=(jax.ShapeDtypeStruct((64, HEADS * KVL),...]
    dot_general x16 -> x0, matrix products: 62.9 us -> none  [the longest x6 33.8 us: absorb_block(): jnp.einsum('qhk,kc->qhc', weights.astype(jnp.bfloat16), key_rows[:, :late...]
    all_to_all x3 -> x0, waiting for transfers between devices: 53.6 us -> none  [the longest x1 24.6 us: body(): lax.all_to_all(ordered.reshape(groups, -1, row_width), 'dp', split_axis=0...]
    all_to_all x3 -> x0, starting transfers between devices: 32 us -> none  [the longest x1 13.3 us: body(): lax.all_to_all(paired, 'dp', split_axis=0, concat_axis=0, tiled=True)]
    gather x3 -> x0, local copies, waits for them, and re-layouts: 17.4 us -> none  [the longest x2 15.1 us: body(): jnp.take(lax.all_gather(arrived, 'mp', axis=1, tiled=True), source, axis=0)]
    all_gather x1 -> x0, waiting for transfers between devices: 16.3 us -> none  [body(): lax.all_gather(arrived, 'mp', axis=1, tiled=True)]
    psum x1 -> x0, waiting for transfers between devices: 16.1 us -> none  [body(): preacts = lax.psum(preacts.astype(jnp.bfloat16), 'mp').astype(jnp.float32)]
    unnamed x48 -> x4, local copies, waits for them, and re-layouts: 18.1 us -> 3.78 us
  transfers between devices with their start and end apart: 5 -> 0, of which waited for: 5 -> 0; matrix products, arithmetic and copies ran while one was open for 15% -> 0% of each run, Pallas kernels for 0% -> 0%
where the time goes in v1:
time: 98.6 us; the launch traced here: 98.4 us
  Pallas kernels  93.3 us (95%)
  local copies, waits for them, and re-layouts  3.78 us (4%)
  between operations  1.3 us (1%)
    pallas_call x1, Pallas kernels, body(): pl.pallas_call(kernel, out_shape=(jax.ShapeDtypeStruct((64, HEADS * KVL),...  93.3 us
    unnamed x4, local copies, waits for them, and re-layouts  3.78 us

profile of v1, /device:TPU:1, one launch (start us, length us, event | category | flops | bytes accessed | tf_op | source)
XLA Modules:
  0.0 98.4 jit_solution(7715925536567285228)
XLA Ops:
  1.3 93.3 %prefill.1 = (bf16[64,16384]{1,0:T(8,128)(2,1)}, bf16[64,1792]{1,0:T(8,128)(2,1)}) custom-call(bf16[64,9216]{1,0:T(8,128)(2,1)} %pool_h.1, s32[1,64]{1,0:T(1,128)} %slots_s.1, s32[1,40]{1,0:T(1,128)} %source_v.1, s32[1]{0:T(128)S(6)} %copy.16.pages_s, bf16[64,18432]{1,0:T(8,128)(2,1)} %queries_h.1, bf16[64,576]{1,0:T(8,128)(2,1)} %suffix_v.1, ...), custom_call_target="tpu_custom_call" | custom-call | tf_op jit(solution)/shard_map/prefill/pallas_call | solution.py:542
  94.6 0.0 copy-start
  94.6 3.1 %copy.17 = bf16[64,16384]{1,0:T(8,128)(2,1)} copy(bf16[64,16384]{1,0:T(8,128)(2,1)} %get-tuple-element.4) | data formatting | bytes 4194304
  97.7 0.0 copy-done
  97.7 0.7 copy.18
Async XLA Ops:
  94.6 3.1 %copy-start = (bf16[64,1792]{1,0:T(8,128)(2,1)S(1)}, bf16[64,1792]{1,0:T(8,128)(2,1)}, u32[]{:S(2)}) copy-start(bf16[64,1792]{1,0:T(8,128)(2,1)} %get-tuple-element.5) | copy-start | bytes 688132

commit v2 on v1

--- a/solution.py
+++ b/solution.py
@@ -28,6 +28,7 @@
 GAIN = 192 ** (-0.5) * 1.4426950408889634
 FIRST = 16
 STEP = 4
+PRE = 1
 
 
 def dot(a, b):
@@ -137,20 +138,15 @@
     picked = dot(select.astype(BF), halves)
     disp[...] = picked.reshape(CHIPS, 8, HALF).astype(BF)
 
-    pl.semaphore_wait(barrier, CHIPS + 3)
-
     def disp_copy(k, q):
         return pltpu.make_async_remote_copy(
-            src_ref=disp.at[q], dst_ref=got.at[core, chip], send_sem=disp_ss.at[k], recv_sem=disp_rs.at[k],
+            src_ref=disp.at[q], dst_ref=got.at[core, k], send_sem=disp_ss.at[k], recv_sem=disp_rs.at[k],
             device_id=(q * 2 + core, mp), device_id_type=MESH,
         )
 
     def disp_start(k, carry):
         disp_copy(k, to_chip(k)).start()
         return carry
-
-    lax.fori_loop(1, CHIPS, disp_start, 0)
-    got[core, chip] = disp[chip]
 
     load_pool.wait()
     perm_row = iota((256, 256), 0)
@@ -186,15 +182,15 @@
         send_p[q, 64:80, :] = jnp.where(low_lane, tmp_rope[first], tmp_rope[second])
         send_p[q, 80:144, :] = tmp_lat[second]
 
+    def fill(q, carry):
+        page_fill(q)
+        return carry
+
     def page_start(k, carry):
-        q = to_chip(k)
-        page_fill(q)
-        page_copy(k, q).start()
-        return carry
-
-    lax.fori_loop(1, CHIPS, page_start, 0)
-    page_fill(chip)
-    arr[chip] = send_p[chip]
+        page_copy(k, to_chip(k)).start()
+        return carry
+
+    lax.fori_loop(0, CHIPS, fill, 0)
 
     load_q.wait()
     zeros = jnp.zeros((64, 64), BF)
@@ -224,6 +220,13 @@
         return carry
 
     lax.fori_loop(0, ROWS // BLK, suffix_block, 0)
+
+    pl.semaphore_wait(barrier, CHIPS + 3)
+    lax.fori_loop(1, PRE, page_start, 0)
+    lax.fori_loop(1, CHIPS, disp_start, 0)
+    lax.fori_loop(PRE, CHIPS, page_start, 0)
+    got[core, 0] = disp[chip]
+    arr[chip] = send_p[chip]
 
     def forward_copy(k, q):
         return pltpu.make_async_remote_copy(
@@ -308,6 +311,18 @@
         near_copy(ch, 3).wait_recv()
         far_copy(ch, 3).start()
 
+    def store_copy(b):
+        span = BLK // 64 * KVL
+        cols = slice(b * span, b * span + span)
+        return pltpu.make_async_copy(out.at[:, cols], context_h.at[:, cols], ld.at[5 + b])
+
+    def finish(b):
+        for h in range(b * BLK // 64, (b + 1) * BLK // 64):
+            rows = slice(h * 64, h * 64 + 64)
+            whole = jnp.sum(total[rows, :], axis=1, keepdims=True)
+            out[:, h * KVL : h * KVL + KVL] = (acc[rows, :] / whole).astype(BF)
+        store_copy(b).start()
+
     def attend_chunk(ch):
         far_copy(ch, 1).wait_recv()
         far_copy(ch, 3).wait_recv()
@@ -323,171 +338,208 @@
         bias_a = bias(0)
         bias_b = bias(4)
 
-        def block(b, carry):
-            rows = pl.ds(pl.multiple_of(b * BLK, BLK), BLK)
+        def scores(b):
+            rows = slice(b * BLK, b * BLK + BLK)
             s_a = dot_nt(q_a[rows, :], keys[ch, :, 0:640]) * GAIN + bias_a
             s_b = dot_nt(q_b[rows, :], keys[ch, :, 512:1152]) * GAIN + bias_b
-            old = peak[rows, 0:1]
-            top = jnp.maximum(jnp.max(jnp.maximum(s_a, s_b), axis=1, keepdims=True), old)
+            return s_a, s_b
+
+        def absorb(b, s_a, s_b):
+            rows = slice(b * BLK, b * BLK + BLK)
+            old = peak[rows, :]
+            top = jnp.maximum(s_a, s_b)
+            top = jnp.max(jnp.maximum(top[:, 0:128], top[:, 128:256]), axis=1, keepdims=True)
+            top = jnp.maximum(jnp.broadcast_to(top, (BLK, 128)), old)
             factor = jnp.exp2(old - top)
-            w_a = jnp.exp2(s_a - top)
-            w_b = jnp.exp2(s_b - top)
+            top2 = jnp.concatenate([top, top], axis=1)
+            w_a = jnp.exp2(s_a - top2)
+            w_b = jnp.exp2(s_b - top2)
             both = w_a + w_b
-            peak[rows, :] = jnp.broadcast_to(top, (BLK, 128))
+            peak[rows, :] = top
             total[rows, :] = total[rows, :] * factor + both[:, 0:128] + both[:, 128:256]
-            acc[rows, :] = (
-                acc[rows, :] * factor
-                + dot(w_a.astype(BF), keys[ch, :, 0:KVL])
-                + dot(w_b.astype(BF), keys[ch, :, 640 : 640 + KVL])
-            )
+            w = jnp.concatenate([w_a.astype(BF), w_b.astype(BF)], axis=1)
+            v = jnp.concatenate([keys[ch, :, 0:KVL], keys[ch, :, 640 : 640 + KVL]], axis=0)
+            acc[rows, :] = acc[rows, :] * jnp.concatenate([factor] * 4, axis=1) + dot(w, v)
+
+        blocks = ROWS // BLK
+        now = scores(0)
+        for b in range(blocks):
+            later = scores(b + 1) if b + 1 < blocks else None
+            absorb(b, *now)
+            now = later
+            if ch == CHUNKS - 1:
+                finish(b)
+
+    half = CHIPS // 2
+
+    def got_copy(k):
+        return pltpu.make_async_remote_copy(
+            src_ref=got.at[core, k], dst_ref=got.at[core, k], send_sem=sib_ss.at[k], recv_sem=sib_rs.at[k],
+            device_id=sibling, device_id_type=MESH,
+        )
+
+    def disp_arrive(k, carry):
+        disp_copy(k, to_chip(k)).wait_recv()
+        got_copy(k).start()
+        return carry
+
+    def got_wait(k, carry):
+        got_copy(k).wait_recv()
+        return carry
+
+    def sum_copy(n, step):
+        there = lax.rem(mp + step, 4)
+        return pltpu.make_async_remote_copy(
+            src_ref=part.at[n, pl.ds(pl.multiple_of(there * 32, 32), 32)], dst_ref=rsb.at[n, mp],
+            send_sem=x_ss.at[n, step - 1], recv_sem=x_rs.at[n, step - 1], device_id=x_peer(step), device_id_type=MESH,
+        )
+
+    mine32 = pl.ds(pl.multiple_of(mp * 32, 32), 32)
+
+    def hid_copy(n, step):
+        return pltpu.make_async_remote_copy(
+            src_ref=hid.at[n, mine32], dst_ref=hid.at[n, mine32],
+            send_sem=x_ss.at[n, step + 2], recv_sem=x_rs.at[n, step + 2], device_id=x_peer(step), device_id_type=MESH,
+        )
+
+    def part_copy(n):
+        return pltpu.make_async_remote_copy(
+            src_ref=pxs.at[n], dst_ref=pxr.at[n], send_sem=sib_ss.at[CHIPS + n], recv_sem=sib_rs.at[CHIPS + n],
+            device_id=sibling, device_id_type=MESH,
+        )
+
+    def ret_copy(k):
+        return pltpu.make_async_remote_copy(
+            src_ref=ret_s.at[k], dst_ref=ret_r.at[chip], send_sem=ret_ss.at[k], recv_sem=ret_rs.at[k],
+            device_id=(from_chip(k) * 2 + core, mp), device_id_type=MESH,
+        )
+
+    def expert_up(n):
+        if n == 0:
+            got_copy(0).start()
+        lax.fori_loop(max(1, n * half), n * half + half, disp_arrive, 0)
+        if n == 0:
+            load_gu.wait()
+        lax.fori_loop(n * half, n * half + half, got_wait, 0)
+        rows = jnp.concatenate([got[0, n * half : n * half + half], got[1, n * half : n * half + half]], axis=0)
+        rows = rows.astype(F32).reshape(256, HALF).astype(BF)
+        pr = iota((128, 256), 0)
+        pc = iota((128, 256), 1)
+        same = (pr // 4 == pc // 8) & (lax.rem(pr, 4) == lax.rem(pc, 4))
+        left = dot(jnp.where(same & (lax.rem(pc // 4, 2) == 0), 1.0, 0.0).astype(BF), rows).astype(BF)
+        right = dot(jnp.where(same & (lax.rem(pc // 4, 2) == 1), 1.0, 0.0).astype(BF), rows).astype(BF)
+        part[n] = (dot(left, wgu[0:HALF, :]) + dot(right, wgu[HALF : 2 * HALF, :])).astype(BF)
+        for step in (2, 1, 3):
+            sum_copy(n, step).start()
+        rsb[n, mp] = part[n, mine32, :]
+
+    def expert_act(n):
+        for step in (1, 2, 3):
+            sum_copy(n, step).wait_recv()
+        pre = rsb[n, 0].astype(F32) + rsb[n, 1].astype(F32) + rsb[n, 2].astype(F32) + rsb[n, 3].astype(F32)
+        gate = pre[:, 0:512]
+        hid[n, mine32, :] = (gate / (1.0 + jnp.exp(-gate)) * pre[:, 512:1024]).astype(BF)
+        for step in (2, 1, 3):
+            hid_copy(n, step).start()
+
+    def expert_down(n):
+        if n == 0:
+            load_dn.wait()
+        for step in (1, 2, 3):
+            hid_copy(n, step).wait_recv()
+        dr = iota((256, 128), 0)
+        dc = iota((256, 128), 1)
+        twice = jnp.where((dr // 8 == dc // 4) & (lax.rem(dr, 4) == lax.rem(dc, 4)), 1.0, 0.0).astype(BF)
+        doubled = dot(twice, hid[n]).astype(BF)
+        is_left = lax.rem(iota((256, HALF), 0) // 4, 2) == 0
+        both = jnp.where(is_left, dot(doubled, wdn[:, 0:HALF]), dot(doubled, wdn[:, HALF : 2 * HALF]))
+        pf[n] = both.reshape(2, 128, HALF)
+        pxs[n] = pf[n, other].astype(BF)
+        part_copy(n).start()
+
+    def ret_start(k, carry):
+        ret_copy(k).start()
+        return carry
+
+    def expert_back(n):
+        part_copy(n).wait_recv()
+        rows = slice(n * half, n * half + half)
+        ret_s[rows] = (pf[n, core] + pxr[n].astype(F32)).reshape(half, 8, HALF).astype(BF)
+        lax.fori_loop(max(1, n * half), n * half + half, ret_start, 0)
+        if n == 0:
+            ret_r[chip] = ret_s[0]
+
+    def expert_mix():
+        def ret_wait(k, carry):
+            ret_copy(k).wait_recv()
             return carry
 
-        lax.fori_loop(0, ROWS // BLK, block, 0)
-
-    def disp_wait(k, carry):
-        disp_copy(k, to_chip(k)).wait_recv()
-        return carry
-
-    lax.fori_loop(1, CHIPS, disp_wait, 0)
-    got_copy = pltpu.make_async_remote_copy(
-        src_ref=got.at[core], dst_ref=got.at[core], send_sem=sib_ss.at[0], recv_sem=sib_rs.at[0],
-        device_id=sibling, device_id_type=MESH,
-    )
-    got_copy.start()
-    load_gu.wait()
-    got_copy.wait_recv()
-    rows512 = got[...].astype(F32).reshape(512, HALF).astype(BF)
-    pr = iota((256, 512), 0)
-    pc = iota((256, 512), 1)
-    same = (pr // 4 == pc // 8) & (lax.rem(pr, 4) == lax.rem(pc, 4))
-    left = dot(jnp.where(same & (lax.rem(pc // 4, 2) == 0), 1.0, 0.0).astype(BF), rows512).astype(BF)
-    right = dot(jnp.where(same & (lax.rem(pc // 4, 2) == 1), 1.0, 0.0).astype(BF), rows512).astype(BF)
-    part[...] = (dot(left, wgu[0:HALF, :]) + dot(right, wgu[HALF : 2 * HALF, :])).astype(BF)
-
-    def sum_copy(step):
-        there = lax.rem(mp + step, 4)
-        return pltpu.make_async_remote_copy(
-            src_ref=part.at[pl.ds(pl.multiple_of(there * 64, 64), 64)], dst_ref=rsb.at[mp],
-            send_sem=x_ss.at[step - 1], recv_sem=x_rs.at[step - 1], device_id=x_peer(step), device_id_type=MESH,
-        )
-
-    for step in (2, 1, 3):
-        sum_copy(step).start()
-    rsb[mp] = part[mine, :]
-
+        lax.fori_loop(1, CHIPS, ret_wait, 0)
+        rows256 = ret_r[...].astype(F32).reshape(256, HALF).astype(BF)
+        weights = mixw[...]
+        high = weights.astype(BF)
+        low = (weights - high.astype(F32)).astype(BF)
+        dims = (((0,), (0,)), ((), ()))
+        mixed = lax.dot_general(high, rows256, dims, preferred_element_type=F32) + lax.dot_general(
+            low, rows256, dims, preferred_element_type=F32
+        )
+        moe_v[:, 0:HALF] = mixed[0:64].astype(BF)
+        moe_v[:, HALF : 2 * HALF] = mixed[64:128].astype(BF)
+
+
+    order_copy.wait()
+    expert_up(0)
+    expert_up(1)
+    expert_act(0)
+    expert_act(1)
     arrivals(0)
-
-    for step in (1, 2, 3):
-        sum_copy(step).wait_recv()
-    pre = rsb[0].astype(F32) + rsb[1].astype(F32) + rsb[2].astype(F32) + rsb[3].astype(F32)
-    gate = pre[:, 0:512]
-    hid[mine, :] = (gate / (1.0 + jnp.exp(-gate)) * pre[:, 512:1024]).astype(BF)
-
-    def hid_copy(step):
-        return pltpu.make_async_remote_copy(
-            src_ref=hid.at[mine], dst_ref=hid.at[mine],
-            send_sem=x_ss.at[step + 2], recv_sem=x_rs.at[step + 2], device_id=x_peer(step), device_id_type=MESH,
-        )
-
-    for step in (2, 1, 3):
-        hid_copy(step).start()
-
-    order_copy.wait()
     gather_chunk(0)
-
-    for step in (1, 2, 3):
-        hid_copy(step).wait_recv()
-    load_dn.wait()
-    dr = iota((512, 256), 0)
-    dc = iota((512, 256), 1)
-    twice = jnp.where((dr // 8 == dc // 4) & (lax.rem(dr, 4) == lax.rem(dc, 4)), 1.0, 0.0).astype(BF)
-    doubled = dot(twice, hid[...]).astype(BF)
-    is_left = lax.rem(iota((512, HALF), 0) // 4, 2) == 0
-    pf[...] = jnp.where(is_left, dot(doubled, wdn[:, 0:HALF]), dot(doubled, wdn[:, HALF : 2 * HALF])).reshape(2, 256, HALF)
-    pxs[...] = pf[other].astype(BF)
-    part_copy = pltpu.make_async_remote_copy(
-        src_ref=pxs, dst_ref=pxr, send_sem=sib_ss.at[1], recv_sem=sib_rs.at[1], device_id=sibling, device_id_type=MESH,
-    )
-    part_copy.start()
-
     arrivals(1)
-    part_copy.wait_recv()
-    ret_s[...] = (pf[core] + pxr[...].astype(F32)).reshape(CHIPS, 8, HALF).astype(BF)
-
-    def ret_copy(k, q):
-        return pltpu.make_async_remote_copy(
-            src_ref=ret_s.at[q], dst_ref=ret_r.at[chip], send_sem=ret_ss.at[k], recv_sem=ret_rs.at[k],
-            device_id=(q * 2 + core, mp), device_id_type=MESH,
-        )
-
-    def ret_start(k, carry):
-        ret_copy(k, to_chip(k)).start()
-        return carry
-
-    lax.fori_loop(1, CHIPS, ret_start, 0)
-    ret_r[chip] = ret_s[chip]
-
     gather_chunk(1)
-    relay_chunk(0)
+    expert_down(0)
     arrivals(2)
     gather_chunk(2)
-    relay_chunk(1)
+    expert_down(1)
+    relay_chunk(0)
     arrivals(3)
     gather_chunk(3)
-    attend_chunk(0)
-    relay_chunk(2)
+    relay_chunk(1)
     arrivals(4)
     gather_chunk(4)
+    relay_chunk(2)
+    expert_back(0)
+    expert_back(1)
+    attend_chunk(0)
+    relay_chunk(3)
     attend_chunk(1)
-    relay_chunk(3)
+    relay_chunk(4)
     attend_chunk(2)
-    relay_chunk(4)
     attend_chunk(3)
-
-    def ret_wait(k, carry):
-        ret_copy(k, to_chip(k)).wait_recv()
-        return carry
-
-    lax.fori_loop(1, CHIPS, ret_wait, 0)
-    rows256 = ret_r[...].astype(F32).reshape(256, HALF).astype(BF)
-    weights = mixw[...]
-    high = weights.astype(BF)
-    low = (weights - high.astype(F32)).astype(BF)
-    dims = (((0,), (0,)), ((), ()))
-    mixed = lax.dot_general(high, rows256, dims, preferred_element_type=F32) + lax.dot_general(
-        low, rows256, dims, preferred_element_type=F32
-    )
-    moe_v[:, 0:HALF] = mixed[0:64].astype(BF)
-    moe_v[:, HALF : 2 * HALF] = mixed[64:128].astype(BF)
-
     attend_chunk(4)
-
-    for h in range(HEADS):
-        rows = slice(h * 64, h * 64 + 64)
-        whole = jnp.sum(total[rows, :], axis=1, keepdims=True)
-        out[:, h * KVL : h * KVL + KVL] = (acc[rows, :] / whole).astype(BF)
-    store = pltpu.make_async_copy(out, context_h, ld.at[5])
-    store.start()
+    expert_mix()
 
     def sent(k, carry):
         disp_copy(k, to_chip(k)).wait_send()
         page_copy(k, to_chip(k)).wait_send()
         forward_copy(k, from_chip(k)).wait_send()
-        ret_copy(k, to_chip(k)).wait_send()
+        ret_copy(k).wait_send()
+        got_copy(k).wait_send()
         return carry
 
     lax.fori_loop(1, CHIPS, sent, 0)
     forward_copy(0, chip).wait_send()
-    got_copy.wait_send()
-    part_copy.wait_send()
-    for step in (1, 2, 3):
-        sum_copy(step).wait_send()
-        hid_copy(step).wait_send()
+    got_copy(0).wait_send()
+    for n in range(2):
+        part_copy(n).wait_send()
+        for step in (1, 2, 3):
+            sum_copy(n, step).wait_send()
+            hid_copy(n, step).wait_send()
     for ch in range(CHUNKS):
         for step in (1, 3):
             near_copy(ch, step).wait_send()
             far_copy(ch, step).wait_send()
-    store.wait()
+    for b in range(ROWS // BLK):
+        store_copy(b).wait()
 
 
 def body(
@@ -519,23 +571,23 @@
         pltpu.VMEM((512, 2 * HALF), BF),
         pltpu.VMEM((CHIPS, 8, HALF), BF),
         pltpu.VMEM((2, CHIPS, 8, HALF), BF),
-        pltpu.VMEM((256, 1024), BF),
-        pltpu.VMEM((4, 64, 1024), BF),
-        pltpu.VMEM((256, 512), BF),
-        pltpu.VMEM((2, 256, HALF), F32),
-        pltpu.VMEM((256, HALF), BF),
-        pltpu.VMEM((256, HALF), BF),
+        pltpu.VMEM((2, 128, 1024), BF),
+        pltpu.VMEM((2, 4, 32, 1024), BF),
+        pltpu.VMEM((2, 128, 512), BF),
+        pltpu.VMEM((2, 2, 128, HALF), F32),
+        pltpu.VMEM((2, 128, HALF), BF),
+        pltpu.VMEM((2, 128, HALF), BF),
         pltpu.VMEM((CHIPS, 8, HALF), BF),
         pltpu.VMEM((CHIPS, 8, HALF), BF),
         pltpu.VMEM((256, 128), F32),
         pltpu.VMEM((8, 128), I32),
         pltpu.SMEM((8, 128), I32),
-        dma((6,)),
+        dma((9,)),
         dma((CHIPS,)), dma((CHIPS,)),
         dma((CHIPS,)), dma((CHIPS,)),
         dma((CHIPS,)), dma((CHIPS,)),
-        dma((2,)), dma((2,)),
-        dma((6,)), dma((6,)),
+        dma((CHIPS + 2,)), dma((CHIPS + 2,)),
+        dma((2, 6)), dma((2, 6)),
         dma((CHIPS,)), dma((CHIPS,)),
         dma((CHUNKS, 4)), dma((CHUNKS, 4)),
     ]

time: 98.6 us -> 88.5 us (0.90)
  Pallas kernels: 93.3 us -> 83.3 us
    pallas_call x1, Pallas kernels: 93.3 us -> 83.3 us  [body(): pl.pallas_call(kernel, out_shape=(jax.ShapeDtypeStruct((64, HEADS * KVL),...]
where the time goes in v2:
time: 88.5 us; the launch traced here: 88.3 us
  Pallas kernels  83.3 us (94%)
  local copies, waits for them, and re-layouts  3.78 us (4%)
  between operations  1.3 us (1%)
    pallas_call x1, Pallas kernels, body(): pl.pallas_call(kernel, out_shape=(jax.ShapeDtypeStruct((64, HEADS * KVL),...  83.3 us
    unnamed x4, local copies, waits for them, and re-layouts  3.78 us

profile of v2, /device:TPU:1, one launch (start us, length us, event | category | flops | bytes accessed | tf_op | source)
XLA Modules:
  0.0 88.3 jit_solution(6008131604145446591)
XLA Ops:
  1.3 83.3 %prefill.1 = (bf16[64,16384]{1,0:T(8,128)(2,1)}, bf16[64,1792]{1,0:T(8,128)(2,1)}) custom-call(bf16[64,9216]{1,0:T(8,128)(2,1)} %pool_h.1, s32[1,64]{1,0:T(1,128)} %slots_s.1, s32[1,40]{1,0:T(1,128)} %source_v.1, s32[1]{0:T(128)S(6)} %copy.16.pages_s, bf16[64,18432]{1,0:T(8,128)(2,1)} %queries_h.1, bf16[64,576]{1,0:T(8,128)(2,1)} %suffix_v.1, ...), custom_call_target="tpu_custom_call" | custom-call | tf_op jit(solution)/shard_map/prefill/pallas_call | solution.py:594
  84.6 0.0 copy-start
  84.6 3.1 %copy.17 = bf16[64,16384]{1,0:T(8,128)(2,1)} copy(bf16[64,16384]{1,0:T(8,128)(2,1)} %get-tuple-element.4) | data formatting | bytes 4194304
  87.7 0.0 copy-done
  87.7 0.7 copy.18
Async XLA Ops:
  84.6 3.1 %copy-start = (bf16[64,1792]{1,0:T(8,128)(2,1)S(1)}, bf16[64,1792]{1,0:T(8,128)(2,1)}, u32[]{:S(2)}) copy-start(bf16[64,1792]{1,0:T(8,128)(2,1)} %get-tuple-element.5) | copy-start | bytes 688132

commit v3 on v2

--- a/solution.py
+++ b/solution.py
@@ -81,7 +81,7 @@
         pl.semaphore_signal(barrier, inc=1, device_id=(to_chip(k) * 2 + core, mp), device_id_type=MESH)
         return carry
 
-    lax.fori_loop(1, CHIPS, greet, 0)
+    lax.fori_loop(1, CHIPS, greet, 0, unroll=True)
     pl.semaphore_signal(barrier, inc=1, device_id=sibling, device_id_type=MESH)
     for step in (1, 2, 3):
         pl.semaphore_signal(barrier, inc=1, device_id=x_peer(step), device_id_type=MESH)
@@ -222,9 +222,9 @@
     lax.fori_loop(0, ROWS // BLK, suffix_block, 0)
 
     pl.semaphore_wait(barrier, CHIPS + 3)
-    lax.fori_loop(1, PRE, page_start, 0)
-    lax.fori_loop(1, CHIPS, disp_start, 0)
-    lax.fori_loop(PRE, CHIPS, page_start, 0)
+    lax.fori_loop(1, PRE, page_start, 0, unroll=True)
+    lax.fori_loop(1, CHIPS, disp_start, 0, unroll=True)
+    lax.fori_loop(PRE, CHIPS, page_start, 0, unroll=True)
     got[core, 0] = disp[chip]
     arr[chip] = send_p[chip]
 
@@ -496,19 +496,19 @@
     gather_chunk(0)
     arrivals(1)
     gather_chunk(1)
-    expert_down(0)
     arrivals(2)
     gather_chunk(2)
+    expert_down(0)
+    relay_chunk(0)
     expert_down(1)
-    relay_chunk(0)
     arrivals(3)
     gather_chunk(3)
     relay_chunk(1)
     arrivals(4)
     gather_chunk(4)
-    relay_chunk(2)
     expert_back(0)
     expert_back(1)
+    relay_chunk(2)
     attend_chunk(0)
     relay_chunk(3)
     attend_chunk(1)

time: 88.5 us -> 87.9 us (level)
  no operation moved by 1% of the time
where the time goes in v3:
time: 87.9 us; the launch traced here: 87.8 us
  Pallas kernels  82.7 us (94%)
  local copies, waits for them, and re-layouts  3.78 us (4%)
  between operations  1.3 us (1%)
    pallas_call x1, Pallas kernels, body(): pl.pallas_call(kernel, out_shape=(jax.ShapeDtypeStruct((64, HEADS * KVL),...  82.7 us
    unnamed x4, local copies, waits for them, and re-layouts  3.78 us

profile of v3, /device:TPU:1, one launch (start us, length us, event | category | flops | bytes accessed | tf_op | source)
XLA Modules:
  0.0 87.8 jit_solution(2899716102536557820)
XLA Ops:
  1.3 82.7 %prefill.1 = (bf16[64,16384]{1,0:T(8,128)(2,1)}, bf16[64,1792]{1,0:T(8,128)(2,1)}) custom-call(bf16[64,9216]{1,0:T(8,128)(2,1)} %pool_h.1, s32[1,64]{1,0:T(1,128)} %slots_s.1, s32[1,40]{1,0:T(1,128)} %source_v.1, s32[1]{0:T(128)S(6)} %copy.16.pages_s, bf16[64,18432]{1,0:T(8,128)(2,1)} %queries_h.1, bf16[64,576]{1,0:T(8,128)(2,1)} %suffix_v.1, ...), custom_call_target="tpu_custom_call" | custom-call | tf_op jit(solution)/shard_map/prefill/pallas_call | solution.py:594
  84.0 0.0 copy-start
  84.0 3.1 %copy.17 = bf16[64,16384]{1,0:T(8,128)(2,1)} copy(bf16[64,16384]{1,0:T(8,128)(2,1)} %get-tuple-element.4) | data formatting | bytes 4194304
  87.1 0.0 copy-done
  87.1 0.7 copy.18
Async XLA Ops:
  84.0 3.1 %copy-start = (bf16[64,1792]{1,0:T(8,128)(2,1)S(1)}, bf16[64,1792]{1,0:T(8,128)(2,1)}, u32[]{:S(2)}) copy-start(bf16[64,1792]{1,0:T(8,128)(2,1)} %get-tuple-element.5) | copy-start | bytes 688132
